TPU v7x, 32 devices: a whole 2x2x4 slice. The times are simulated.
32 devices in a mesh: dp: 8 (over z, core), ctx: 4 (over y, x).
Axes of the slice: x: 2, y: 2, z: 4, core: 2. Of those that a mesh axis runs over, the one named last changes fastest.
Arguments:
- query_rows: bfloat16 [1536, 8, 640], P(('dp', 'ctx')), parts along dimension 0, may hold values from -6 to 6
- key_rows: bfloat16 [1536, 8, 640], P(('dp', 'ctx')), parts along dimension 0, may hold values from -6 to 6
- value_rows: bfloat16 [1536, 8, 640], P(('dp', 'ctx')), parts along dimension 0, may hold values from -6 to 6
- token_rates: bfloat16 [1536, 8], P(('dp', 'ctx')), parts along dimension 0, may hold values from 0.099609375 to 1
- fast_weights: float32 [8, 3, 640, 1280], P('ctx'), may hold values from -0.25 to 0.25
Outputs:
- outputs: bfloat16 [1536, 8, 640], P(('dp', 'ctx')), parts along dimension 0
- new_weights: float32 [64, 3, 640, 1280], P(('dp', 'ctx')), parts along dimension 0
There are 8 independent parts, one for each index of `dp`. A program takes and returns all parts, laid end to end along the dimension named above; an argument that names none is the same for every part. Nothing has to cross between parts.
All inputs are finite; a program needn't handle non-finite values.
Results may differ from a plain program's by a relative error of at most 0.019.
Values may be sent and summed in bfloat16 or wider, within the bound.
A program may use at most 192 MiB of HBM per device.

v0:
```python
import math

import jax
import jax.numpy as jnp
from jax import lax
from jax.sharding import PartitionSpec as P

NS_ITERS = 3


linear_term = 3.4445
cubic_term = -4.775
quintic_term = 2.0315


def split_blocks(rows, block_count):
    return rows.reshape(block_count, rows.shape[0] // block_count, rows.shape[-1])


def block_sum(left, right):
    partial_terms = jnp.einsum(
        "ntd,nth->ndh", left, right, preferred_element_type=jnp.float32
    ).astype(jnp.bfloat16)
    partial_terms = lax.optimization_barrier(partial_terms)
    return jnp.sum(partial_terms.astype(jnp.float32), axis=0)


def orthogonal(grad_matrix, iterations):
    ortho = (grad_matrix * lax.rsqrt(jnp.sum(grad_matrix * grad_matrix) + 1e-06)).astype(
        jnp.bfloat16
    )
    for _ in range(iterations):
        gram = jnp.dot(ortho, ortho.T, preferred_element_type=jnp.float32).astype(jnp.bfloat16)
        square = jnp.dot(gram, gram, preferred_element_type=jnp.float32)
        combined = (cubic_term * gram.astype(jnp.float32) + quintic_term * square).astype(
            jnp.bfloat16
        )
        mixed = jnp.dot(combined, ortho, preferred_element_type=jnp.float32)
        ortho = (linear_term * ortho.astype(jnp.float32) + mixed).astype(jnp.bfloat16)
    return ortho


def head_update(key_head, value_head, rate_head, weights_head, block_count):
    weights_bf = weights_head.astype(jnp.bfloat16)
    gate_pre = jnp.dot(key_head, weights_bf[0], preferred_element_type=jnp.float32)
    up_proj = jnp.dot(key_head, weights_bf[1], preferred_element_type=jnp.float32)
    sigmoid_gate = jax.nn.sigmoid(gate_pre)
    silu_gate = gate_pre * sigmoid_gate
    hidden = (silu_gate * up_proj).astype(jnp.bfloat16)
    scaled = (rate_head.astype(jnp.float32)[:, None] * value_head.astype(jnp.float32)).astype(
        jnp.bfloat16
    )
    back_grad = -jnp.dot(scaled, weights_bf[2], preferred_element_type=jnp.float32)
    grad_gate = (
        back_grad * up_proj * sigmoid_gate * (1.0 + gate_pre * (1.0 - sigmoid_gate))
    ).astype(jnp.bfloat16)
    grad_up = (back_grad * silu_gate).astype(jnp.bfloat16)
    key_blocks = split_blocks(key_head, block_count)
    first = block_sum(key_blocks, split_blocks(grad_gate, block_count))
    second = block_sum(key_blocks, split_blocks(grad_up, block_count))
    third = -block_sum(split_blocks(scaled, block_count), split_blocks(hidden, block_count))
    step_scale = math.sqrt(weights_head.shape[-2] / weights_head.shape[-1])
    updated = []
    for index, grad_matrix in enumerate([first, second, third]):
        updated.append(
            weights_head[index] - step_scale * orthogonal(grad_matrix, NS_ITERS).astype(jnp.float32)
        )
    return jnp.stack(updated)


def apply_head(query_head, weights_bf):
    gate_pre = jnp.dot(query_head, weights_bf[0], preferred_element_type=jnp.float32)
    up_proj = jnp.dot(query_head, weights_bf[1], preferred_element_type=jnp.float32)
    hidden = (jax.nn.silu(gate_pre) * up_proj).astype(jnp.bfloat16)
    result = lax.dot_general(
        hidden, weights_bf[2], (((1,), (1,)), ((), ())), preferred_element_type=jnp.float32
    )
    return result.astype(jnp.bfloat16)


def owner_weights(key_moved, value_moved, rate_moved, fast_weights, block_count):
    updated = []
    for local in range(fast_weights.shape[0]):
        updated.append(
            head_update(
                key_moved[:, local, :],
                value_moved[:, local, :],
                rate_moved[:, local],
                fast_weights[local],
                block_count,
            )
        )
    return jnp.stack(updated)


def body(query_rows, key_rows, value_rows, token_rates, fast_weights):
    ctx_count = lax.axis_size("ctx")
    key_moved, value_moved, rate_moved = (
        lax.all_to_all(key_rows, "ctx", split_axis=1, concat_axis=0, tiled=True),
        lax.all_to_all(value_rows, "ctx", split_axis=1, concat_axis=0, tiled=True),
        lax.all_to_all(token_rates, "ctx", split_axis=1, concat_axis=0, tiled=True),
    )
    new_weights = owner_weights(key_moved, value_moved, rate_moved, fast_weights, ctx_count)
    applied = new_weights.astype(jnp.bfloat16)
    piece = lax.all_gather(applied, "ctx", axis=0, tiled=True)
    count = piece.shape[0]
    pieces = [apply_head(query_rows[:, index, :], piece[index]) for index in range(count)]
    outputs = jnp.stack(pieces, axis=1)
    return (outputs, new_weights)


def solution(mesh):
    placed = (
        P(("dp", "ctx"), None, None),
        P(("dp", "ctx"), None, None),
        P(("dp", "ctx"), None, None),
        P(("dp", "ctx"), None),
        P("ctx", None, None, None),
    )
    return jax.shard_map(
        body,
        mesh=mesh,
        in_specs=placed,
        out_specs=(P(("dp", "ctx"), None, None), P(("dp", "ctx"), None, None, None)),
        check_vma=False,
    )
```

profile of v0, /device:TPU:0, one launch (start us, length us, event | category | flops | bytes accessed | tf_op | source)
XLA Modules:
  0.0 670.0 jit_solution(14583036460385035035)
XLA Ops:
  7.2 5.3 all-to-all-start
  17.1 3.5 all-to-all-start.1
  21.4 5.7 all-to-all-done.1
  27.1 3.5 all-to-all-start.2
  30.6 11.5 %convert.6 = bf16[2,3,640,1280]{3,2,1,0:T(8,128)(2,1)} convert(f32[2,3,640,1280]{3,2,1,0:T(8,128)} %param.9) | non-fusion elementwise | flops 4915200 | bytes 29491200 | tf_op jit(solution)/shard_map/convert.3
  89.0 5.4 convolution_convert_fusion.10
  94.5 5.3 fusion.15
  99.7 4.4 convolution_convert_fusion.9
  104.1 4.1 fusion.16
  111.7 7.7 %fusion.2 = f32[1,640,1280]{2,1,0:T(8,128)} fusion(f32[2,3,640,1280]{3,2,1,0:T(8,128)} %param.9, bf16[640,1280]{1,0:T(8,128)(2,1)} %copy-done.19, bf16[640,640]{1,0:T(8,128)(2,1)} %convolution_convert_fusion.8), kind=kOutput, calls=%fused_computation.38 | convolution fusion | flops 1580646400 | bytes 12288000 | tf_op jit(solution)/shard_map/dot_general | solution.py:38
  122.5 5.3 fusion.18
  127.7 3.6 convolution_convert_fusion.6
  131.4 4.2 fusion.19
  137.1 6.1 fusion.1
  150.5 5.2 fusion.21
  155.7 4.8 convolution_convert_fusion.3
  160.5 4.0 fusion.22
  168.0 7.8 %fusion = f32[1,640,1280]{2,1,0:T(8,128)} fusion(f32[2,3,640,1280]{3,2,1,0:T(8,128)} %param.9, bf16[640,1280]{1,0:T(8,128)(2,1)} %copy-done.20, bf16[640,640]{1,0:T(8,128)(2,1)} %convolution_convert_fusion.2), kind=kOutput, calls=%fused_computation.34 | convolution fusion | flops 1580646400 | bytes 12288000 | tf_op jit(solution)/shard_map/dot_general | solution.py:38
  178.9 5.4 fusion.6
  184.3 4.6 convolution_convert_fusion.18
  188.9 4.2 fusion.7
  196.6 8.0 %fusion.5 = f32[1,640,1280]{2,1,0:T(8,128)} fusion(f32[2,3,640,1280]{3,2,1,0:T(8,128)} %param.9, bf16[640,1280]{1,0:T(8,128)(2,1)} %copy-done.21, bf16[640,640]{1,0:T(8,128)(2,1)} %convolution_convert_fusion.17), kind=kOutput, calls=%fused_computation.44 | convolution fusion | flops 1580646400 | bytes 12288000 | tf_op jit(solution)/shard_map/dot_general | solution.py:38
  207.7 5.3 fusion.9
  216.5 4.3 fusion.10
  222.3 6.0 fusion.4
  235.9 5.2 fusion.12
  241.2 4.5 convolution_convert_fusion.12
  245.7 4.0 fusion.13
  253.3 7.8 %fusion.3 = f32[1,640,1280]{2,1,0:T(8,128)} fusion(f32[2,3,640,1280]{3,2,1,0:T(8,128)} %param.9, bf16[640,1280]{1,0:T(8,128)(2,1)} %copy-done.22, bf16[640,640]{1,0:T(8,128)(2,1)} %convolution_convert_fusion.11), kind=kOutput, calls=%fused_computation.40 | convolution fusion | flops 1580646400 | bytes 12288000 | tf_op jit(solution)/shard_map/dot_general | solution.py:38
  261.0 6.4 maximum_bitcast_fusion
  267.4 10.5 %fusion.224 = (bf16[2,3,640,1280]{3,2,1,0:T(8,128)(2,1)}, f32[2,3,640,1280]{3,2,1,0:T(8,128)}) fusion(f32[1,3,640,1280]{3,2,1,0:T(8,128)S(1)} %get-tuple-element.35, f32[1,3,640,1280]{3,2,1,0:T(8,128)S(1)} %get-tuple-element.34), kind=kLoop, calls=%fused_computation.381 | loop fusion | flops 9830400 | bytes 49152000 | tf_op jit(solution)/shard_map/convert_element_type | solution.py:104
  279.8 345.9 %all-gather.2.cloned.1.call-done = bf16[8,3,640,1280]{3,2,1,0:T(8,128)(2,1)} async-done(((bf16[2,3,640,1280]{3,2,1,0:T(8,128)(2,1)}), bf16[8,3,640,1280]{3,2,1,0:T(8,128)(2,1)}) %all-gather.2.cloned.1.call-update) | async-done | bytes 39321616 | tf_op jit(solution)/shard_map/all_gather | solution.py:105
  (128 shorter events, 131.8 us)
Async XLA Ops:
  7.2 13.4 %copy-start.14 = (bf16[48,8,640]{2,1,0:T(8,128)(2,1)S(1)}, bf16[48,8,640]{2,1,0:T(8,128)(2,1)}, u32[]{:S(2)}) copy-start(bf16[48,8,640]{2,1,0:T(8,128)(2,1)} %param.6) | copy-start | bytes 1474564
  7.2 9.9 %all-to-all-start = ((bf16[48,4,2]{0,2,1:T(2,128)(2,1)}), bf16[48,4,2]{0,2,1:T(2,128)(2,1)S(1)}, u32[]{:S(2)}, u32[]{:S(2)}) async-start(bf16[48,4,2]{0,2,1:T(2,128)(2,1)} %bitcast.603), calls=%async_computation | async-start | bytes 4096 | tf_op jit(solution)/shard_map/all_to_all | solution.py:101
  17.1 10.0 %all-to-all-start.1 = ((bf16[48,8,640]{2,0,1:T(8,128)(2,1)}), bf16[48,8,640]{2,0,1:T(8,128)(2,1)S(1)}, u32[]{:S(2)}, u32[]{:S(2)}) async-start(bf16[48,8,640]{2,0,1:T(8,128)(2,1)} %copy.34), calls=%async_computation.1 | async-start | bytes 983040 | tf_op jit(solution)/shard_map/all_to_all | solution.py:100
  27.1 15.4 %all-to-all-start.2 = ((bf16[48,8,640]{2,0,1:T(8,128)(2,1)}), bf16[48,8,640]{2,0,1:T(8,128)(2,1)S(1)}, u32[]{:S(2)}, u32[]{:S(2)}) async-start(bf16[48,8,640]{2,0,1:T(8,128)(2,1)} %copy.36), calls=%async_computation.2 | async-start | bytes 983040 | tf_op jit(solution)/shard_map/all_to_all | solution.py:99
  30.5 595.2 %all-gather.2.cloned.1.call-start = ((), (), s32[]{:S(2)}) async-start(), calls=%async_computation.3 | async-start | bytes 49152000 | tf_op jit(solution)/shard_map/all_gather | solution.py:105
  42.4 2.5 copy-start.12
  42.5 4.4 copy-start
  42.5 7.6 %copy-start.7 = (bf16[192,1,640]{2,0,1:T(8,128)(2,1)}, bf16[192,1,640]{2,0,1:T(8,128)(2,1)S(1)}, u32[]{:S(2)}) copy-start(bf16[192,1,640]{2,0,1:T(8,128)(2,1)S(1)} %get-tuple-element.29) | copy-start | bytes 737284
  56.0 1.5 copy-start.8
  56.0 1.5 copy-start.18
  63.8 1.5 copy-start.13
  63.8 2.5 copy-start.1
  79.5 1.4 copy-start.17
  89.0 5.4 copy-start.6
  99.7 4.4 copy-start.23
  108.2 1.2 copy-start.19
  111.7 8.3 %copy-start.5 = (f32[640,1280]{1,0:T(8,128)S(1)}, f32[640,1280]{1,0:T(8,128)}, u32[]{:S(2)}) copy-start(f32[640,1280]{1,0:T(8,128)} %copy.41) | copy-start | bytes 9830404
  137.0 6.1 copy-start.11
  137.1 6.1 copy-start.16
  155.7 4.8 copy-start.25
  164.5 1.2 copy-start.20
  168.0 8.4 %copy-start.4 = (f32[640,1280]{1,0:T(8,128)S(1)}, f32[640,1280]{1,0:T(8,128)}, u32[]{:S(2)}) copy-start(f32[640,1280]{1,0:T(8,128)} %copy.38) | copy-start | bytes 9830404
  184.3 4.6 copy-start.24
  193.1 1.2 copy-start.21
  196.6 8.7 %copy-start.3 = (f32[640,1280]{1,0:T(8,128)S(1)}, f32[640,1280]{1,0:T(8,128)}, u32[]{:S(2)}) copy-start(f32[640,1280]{1,0:T(8,128)} %copy.39) | copy-start | bytes 9830404
  222.3 6.0 copy-start.10
  222.3 6.0 copy-start.15
  241.2 4.5 copy-start.26
  249.7 1.2 copy-start.22
  253.3 7.8 %copy-start.2 = (f32[1,640,1280]{2,1,0:T(8,128)S(1)}, f32[1,640,1280]{2,1,0:T(8,128)}, u32[]{:S(2)}) copy-start(f32[1,640,1280]{2,1,0:T(8,128)} %fusion.2) | copy-start | bytes 9830404
  277.9 1.0 copy-start.9
Sparse Core Ops, SparseCore 0:
  278.1 347.5 all-gather.1
where the time goes:
time: 678 us; the launch traced here: 670 us
  waiting for transfers between devices  354 us (52%)
  matrix products  217 us (32%)
  other arithmetic  44.1 us (7%)
  local copies, waits for them, and re-layouts  23 us (3%)
  between operations  18.9 us (3%)
  starting transfers between devices  12.3 us (2%)
    all_gather x1, waiting for transfers between devices, body(): piece = lax.all_gather(applied, 'ctx', axis=0, tiled=True)  346 us
    dot_general x18, matrix products, orthogonal(): mixed = jnp.dot(combined, ortho, preferred_element_type=jnp.float32)  99.8 us
    dot_general x18, matrix products, orthogonal(): jnp.dot(ortho, ortho.T, preferred_element_type=jnp.float32)  55.2 us
    dot_general x8, matrix products, apply_head(): lax.dot_general(hidden, weights_bf[2], (((1,), (1,)), ((), ())), preferre...  21.8 us
    dot_general x8, matrix products, apply_head(): jnp.dot(query_head, weights_bf[0], preferred_element_type=jnp.float32)  14.2 us
  transfers between devices with their start and end apart: 4, of which 3 were waited for; matrix products, arithmetic and copies ran while one was open for 2% of the time, Pallas kernels for 0%

commit v1 on v0

v1 whole, which is shorter than its diff:
```python
import math

import jax
import jax.numpy as jnp
from jax import lax
from jax.sharding import PartitionSpec as P

NS_ITERS = 3

linear_term = 3.4445
cubic_term = -4.775
quintic_term = 2.0315


def mm(left, right):
    return jnp.einsum(
        "...ij,...jk->...ik",
        left,
        right,
        precision=lax.Precision.HIGHEST,
        preferred_element_type=jnp.float32,
    )


def gram(rows):
    return jnp.einsum("...ih,...jh->...ij", rows, rows, preferred_element_type=jnp.float32)


def factor_chain(square, key_gram):
    norm = jnp.maximum(jnp.sum(square * key_gram, axis=(-2, -1), keepdims=True), 0.0)
    inverse = lax.rsqrt(norm + 1e-06)
    power = mm(square * (inverse * inverse), key_gram)
    eye = jnp.eye(square.shape[-1], dtype=jnp.float32)
    total = None
    for step in range(NS_ITERS):
        squared = mm(power, power)
        poly = linear_term * eye + cubic_term * power + quintic_term * squared
        total = poly if total is None else mm(poly, total)
        if step < NS_ITERS - 1:
            power = mm(poly, mm(poly, power))
    return total * inverse


def body(query_rows, key_rows, value_rows, token_rates, fast_weights):
    ctx_count = lax.axis_size("ctx")
    local = fast_weights.shape[0]
    tokens, heads, width = key_rows.shape
    scaled = (
        token_rates.astype(jnp.float32)[:, :, None] * value_rows.astype(jnp.float32)
    ).astype(jnp.bfloat16)
    packed = jnp.stack([key_rows, scaled, query_rows]).transpose(2, 0, 1, 3)
    moved = lax.all_to_all(packed, "ctx", split_axis=0, concat_axis=0, tiled=True)
    moved = moved.reshape(ctx_count, local, 3, tokens, width).transpose(1, 2, 0, 3, 4)
    moved = moved.reshape(local, 3, ctx_count * tokens, width)
    keys, scaled, queries = moved[:, 0], moved[:, 1], moved[:, 2]

    weights_bf = fast_weights.astype(jnp.bfloat16)
    dot = lambda a, b: jnp.einsum("ltd,ldh->lth", a, b, preferred_element_type=jnp.float32)
    gate_pre = dot(keys, weights_bf[:, 0])
    up_proj = dot(keys, weights_bf[:, 1])
    back_grad = -dot(scaled, weights_bf[:, 2])
    sigmoid_gate = jax.nn.sigmoid(gate_pre)
    silu_gate = gate_pre * sigmoid_gate
    hidden = (silu_gate * up_proj).astype(jnp.bfloat16)
    grad_gate = (
        back_grad * up_proj * sigmoid_gate * (1.0 + gate_pre * (1.0 - sigmoid_gate))
    ).astype(jnp.bfloat16)
    grad_up = (back_grad * silu_gate).astype(jnp.bfloat16)
    rights = jnp.stack([grad_gate, grad_up, hidden], axis=1)
    key_gram, scaled_gram = gram(keys), gram(scaled)
    lefts_gram = jnp.stack([key_gram, key_gram, scaled_gram], axis=1)
    chain = factor_chain(gram(rights), lefts_gram).astype(jnp.bfloat16)
    mixed = jnp.einsum("lkij,lkjh->lkih", chain, rights, preferred_element_type=jnp.float32)
    mixed = mixed.astype(jnp.bfloat16)
    lefts = jnp.stack([keys, keys, -scaled], axis=1)
    ortho = jnp.einsum("lktd,lkth->lkdh", lefts, mixed, preferred_element_type=jnp.float32)
    step_scale = math.sqrt(fast_weights.shape[-2] / fast_weights.shape[-1])
    new_weights = fast_weights - step_scale * ortho
    applied = new_weights.astype(jnp.bfloat16)

    hidden = (
        jax.nn.silu(dot(queries, applied[:, 0])) * dot(queries, applied[:, 1])
    ).astype(jnp.bfloat16)
    result = jnp.einsum(
        "lth,ldh->ltd", hidden, applied[:, 2], preferred_element_type=jnp.float32
    ).astype(jnp.bfloat16)
    result = result.reshape(local, ctx_count, tokens, width).transpose(1, 0, 2, 3)
    result = result.reshape(heads, tokens, width)
    outputs = lax.all_to_all(result, "ctx", split_axis=0, concat_axis=0, tiled=True)
    return (outputs.transpose(1, 0, 2), new_weights)


def solution(mesh):
    placed = (
        P(("dp", "ctx"), None, None),
        P(("dp", "ctx"), None, None),
        P(("dp", "ctx"), None, None),
        P(("dp", "ctx"), None),
        P("ctx", None, None, None),
    )
    return jax.shard_map(
        body,
        mesh=mesh,
        in_specs=placed,
        out_specs=(P(("dp", "ctx"), None, None), P(("dp", "ctx"), None, None, None)),
        check_vma=False,
    )
```

time: 678 us -> 94.6 us (0.14); the launches traced: 670 us -> 94 us
  waiting for transfers between devices: 354 us -> 18.2 us
  matrix products: 217 us -> 52.3 us
  other arithmetic: 44.1 us -> 4.03 us
  local copies, waits for them, and re-layouts: 23 us -> 3.42 us
  between operations: 18.9 us -> 0.85 us
  blocking collectives: 0 us -> 10.1 us
  starting transfers between devices: 12.3 us -> 5.16 us
    all_gather x1 -> x0, waiting for transfers between devices: 346 us -> none  [body(): piece = lax.all_gather(applied, 'ctx', axis=0, tiled=True)]
    dot_general x64 -> x19, matrix products: 217 us -> 52.3 us  [the longest x1 16.1 us: body(): jnp.einsum('lktd,lkth->lkdh', lefts, mixed, preferred_element_type=jnp.fl...]
    another operation x2 -> x1, other arithmetic: 17.9 us -> 1.18 us  [body(): packed = jnp.stack([key_rows, scaled, query_rows]).transpose(2, 0, 1, 3)]
    reduce_sum x12 -> x0, other arithmetic: 14.7 us -> none  [the longest x6 8.83 us: orthogonal(): jnp.sum(grad_matrix * grad_matrix) + 1e-06]
    reduce_sum x4 -> x0, local copies, waits for them, and re-layouts: 12.5 us -> none  [block_sum(): return jnp.sum(partial_terms.astype(jnp.float32), axis=0)]
    convert_element_type x4 -> x1, other arithmetic: 11.6 us -> 0.68 us  [body(): token_rates.astype(jnp.float32)[:, :, None] * value_rows.astype(jnp.float32)]
    all_to_all x0 -> x1, blocking collectives: none -> 10.1 us  [body(): lax.all_to_all(result, 'ctx', split_axis=0, concat_axis=0, tiled=True)]
    all_to_all x3 -> x1, waiting for transfers between devices: 8.4 us -> 18.2 us  [body(): lax.all_to_all(packed, 'ctx', split_axis=0, concat_axis=0, tiled=True)]
  transfers between devices with their start and end apart: 4 -> 1, of which waited for: 3 -> 1; matrix products, arithmetic and copies ran while one was open for 2% -> 0% of each run, Pallas kernels for 0% -> 0%
where the time goes in v1:
time: 94.6 us; the launch traced here: 94 us
  matrix products  52.3 us (55%)
  waiting for transfers between devices  18.2 us (19%)
  blocking collectives  10.1 us (11%)
  starting transfers between devices  5.16 us (5%)
  other arithmetic  4.03 us (4%)
  local copies, waits for them, and re-layouts  3.42 us (4%)
    all_to_all x1, waiting for transfers between devices, body(): lax.all_to_all(packed, 'ctx', split_axis=0, concat_axis=0, tiled=True)  18.2 us
    dot_general x1, matrix products, body(): jnp.einsum('lktd,lkth->lkdh', lefts, mixed, preferred_element_type=jnp.fl...  16.1 us
    dot_general x4, matrix products, body(): jnp.einsum('ltd,ldh->lth', a, b, preferred_element_type=jnp.float32)  14.9 us
    dot_general x10, matrix products, mm(): jnp.einsum('...ij,...jk->...ik', left, right, precision=lax.Precision.HIG...  13.4 us
    all_to_all x1, blocking collectives, body(): lax.all_to_all(result, 'ctx', split_axis=0, concat_axis=0, tiled=True)  10.1 us
    dot_general x1, matrix products, body(): jnp.einsum('lth,ldh->ltd', hidden, applied[:, 2], preferred_element_type=...  5.72 us
    all_to_all x1, starting transfers between devices, body(): lax.all_to_all(packed, 'ctx', split_axis=0, concat_axis=0, tiled=True)  5.16 us
    dot_general x3, matrix products, gram(): jnp.einsum('...ih,...jh->...ij', rows, rows, preferred_element_type=jnp.f...  2.14 us
  transfers between devices with their start and end apart: 1, of which 1 were waited for; matrix products, arithmetic and copies ran while one was open for 0% of the time, Pallas kernels for 0%

profile of v1, /device:TPU:0, one launch (start us, length us, event | category | flops | bytes accessed | tf_op | source)
XLA Modules:
  0.0 94.0 jit_solution(805226825467681413)
XLA Ops:
  0.6 0.7 convert_element_type.37
  1.3 1.2 %fusion.28 = bf16[1,48,8,640]{3,1,0,2:T(8,128)(2,1)S(1)} fusion(bf16[48,8,640]{2,1,0:T(8,128)(2,1)} %param.7, f32[48,8]{0,1:T(8,128)S(1)} %convert_element_type.37), kind=kLoop, calls=%fused_computation.51 | loop fusion | flops 737280 | bytes 984576 | tf_op jit(solution)/shard_map/stack | solution.py:51
  2.5 1.3 %copy_bitcast_fusion = (bf16[1,48,8,640]{3,1,0,2:T(8,128)(2,1)S(1)}, bf16[1,48,8,640]{3,1,0,2:T(8,128)(2,1)S(1)}) fusion(bf16[48,8,640]{2,1,0:T(8,128)(2,1)} %param.5, bf16[48,8,640]{2,1,0:T(8,128)(2,1)} %param.6), kind=kLoop, calls=%fused_computation.58 | loop fusion | bytes 1966080 | tf_op jit(solution)/shard_map/stack | solution.py:51
  3.8 1.3 %maximum_bitcast_fusion = bf16[8,3,48,640]{3,2,1,0:T(8,128)(2,1)} fusion(bf16[1,48,8,640]{3,1,0,2:T(8,128)(2,1)S(1)} %get-tuple-element.15, bf16[1,48,8,640]{3,1,0,2:T(8,128)(2,1)S(1)} %fusion.28, bf16[1,48,8,640]{3,1,0,2:T(8,128)(2,1)S(1)} %get-tuple-element.16), kind=kLoop, calls=%fused_computation.27 | loop fusion | flops 1474560 | bytes 2949120 | tf_op jit(solution)/shard_map/transpose | solution.py:51
  5.1 5.2 %all-to-all-start = ((bf16[8,3,48,640]{3,2,1,0:T(8,128)(2,1)}), bf16[8,3,48,640]{3,2,1,0:T(8,128)(2,1)S(1)}, u32[]{:S(2)}, u32[]{:S(2)}) async-start(bf16[8,3,48,640]{3,2,1,0:T(8,128)(2,1)} %maximum_bitcast_fusion), calls=%async_computation | async-start | bytes 2949120 | tf_op jit(solution)/shard_map/all_to_all | solution.py:52
  10.3 18.2 %all-to-all-done = bf16[8,3,48,640]{3,2,1,0:T(8,128)(2,1)S(1)} async-done(((bf16[8,3,48,640]{3,2,1,0:T(8,128)(2,1)}), bf16[8,3,48,640]{3,2,1,0:T(8,128)(2,1)S(1)}, u32[]{:S(2)}, u32[]{:S(2)}) %all-to-all-start) | async-done | bytes 1474592 | tf_op jit(solution)/shard_map/all_to_all | solution.py:52
  28.5 0.1 copy.17
  28.6 0.3 convolution_bitcast_fusion.1
  28.9 0.3 convolution_bitcast_fusion
  29.3 0.9 fusion.43
  30.1 3.8 %fusion.3 = f32[2,192,1280]{2,1,0:T(8,128)S(1)} fusion(bf16[2,3,192,640]{3,2,0,1:T(8,128)(2,1)S(1)} %bitcast.101, f32[2,3,640,1280]{3,2,1,0:T(8,128)} %param.9), kind=kOutput, calls=%fused_computation.10 | convolution fusion | flops 629145600 | bytes 5734400 | tf_op jit(solution)/shard_map/ltd,ldh->lth/dot_general | solution.py:58
  33.9 3.8 %fusion.7 = f32[2,192,1280]{2,1,0:T(8,128)S(1)} fusion(bf16[2,3,192,640]{3,2,0,1:T(8,128)(2,1)S(1)} %bitcast.102, f32[2,3,640,1280]{3,2,1,0:T(8,128)} %param.9), kind=kOutput, calls=%fused_computation.16 | convolution fusion | flops 629637120 | bytes 5734400 | tf_op jit(solution)/shard_map/ltd,ldh->lth/dot_general | solution.py:58
  37.7 4.5 %fusion.26 = (bf16[2,1,192,1280]{3,2,0,1:T(8,128)(2,1)S(1)}, bf16[2,1,192,1280]{3,2,0,1:T(8,128)(2,1)S(1)}, bf16[2,1,192,1280]{3,2,0,1:T(8,128)(2,1)S(1)}) fusion(f32[2,192,1280]{2,1,0:T(8,128)S(1)} %fusion.3, f32[2,192,1280]{2,1,0:T(8,128)S(1)} %fusion.7, bf16[2,3,192,640]{3,2,0,1:T(8,128)(2,1)S(1)} %bitcast.103, f32[2,3,640,1280]{3,2,1,0:T(8,128)} %param.9), kind=kOutput, calls=%fused_computation.49 | convolution fusion | flops 636518400 | bytes 10649600 | tf_op jit(solution)/shard_map/ltd,ldh->lth/dot_general | solution.py:58
  42.2 1.5 %multiply_reduce_fusion = (f32[2,3]{1,0:T(2,128)S(1)}, f32[2,3,192,192]{3,2,1,0:T(8,128)S(1)}) fusion(f32[2,1,192,192]{3,2,1,0:T(8,128)S(1)} %convolution_bitcast_fusion, f32[2,1,192,192]{3,2,1,0:T(8,128)S(1)} %convolution_bitcast_fusion.1, bf16[2,1,192,1280]{3,2,0,1:T(8,128)(2,1)S(1)} %get-tuple-element.5, ...), kind=kOutput, calls=%fused_computation.44 | convolution fusion | flops 570064896 | bytes 4423704 | tf_op jit(solution)/shard_map/...ih,...jh->...ij/dot_general | solution.py:26
  43.8 0.0 copy-done.3
  43.8 1.3 %fusion.21 = f32[2,3,192,192]{3,2,1,0:T(8,128)S(1)} fusion(f32[2,3,192,192]{3,2,1,0:T(8,128)S(1)} %get-tuple-element.12, f32[2,1,192,192]{3,2,1,0:T(8,128)S(1)} %convolution_bitcast_fusion, f32[2,1,192,192]{3,2,1,0:T(8,128)S(1)} %convolution_bitcast_fusion.1, f32[2,3]{1,0:T(2,128)S(1)} %get-tuple-element.10), kind=kOutput, calls=%fused_computation.42 | convolution fusion | flops 510271488 | bytes 2359320 | tf_op jit(solution)/shard_map/...ij,...jk->...ik/dot_general | solution.py:16
  45.1 1.4 %fusion.18 = f32[2,3,192,192]{3,2,1,0:T(8,128)S(1)} fusion(f32[2,3,192,192]{3,2,1,0:T(8,128)S(1)} %fusion.21, f32[192,192]{1,0:T(8,128)S(1)} %fusion.36), kind=kOutput, calls=%fused_computation.36 | convolution fusion | flops 510492672 | bytes 1916928 | tf_op jit(solution)/shard_map/...ij,...jk->...ik/dot_general | solution.py:16
  46.5 1.3 %fusion.49 = f32[2,3,192,192]{3,2,1,0:T(8,128)S(1)} fusion(f32[2,3,192,192]{3,2,1,0:T(8,128)S(1)} %fusion.18, f32[2,3,192,192]{3,2,1,0:T(8,128)S(1)} %fusion.21), kind=kOutput, calls=%fused_computation.74 | convolution fusion | flops 509607936 | bytes 2654208 | tf_op jit(solution)/shard_map/...ij,...jk->...ik/dot_general | solution.py:16
  47.8 1.3 %fusion.50 = f32[2,3,192,192]{3,2,1,0:T(8,128)S(1)} fusion(f32[2,3,192,192]{3,2,1,0:T(8,128)S(1)} %fusion.18, f32[2,3,192,192]{3,2,1,0:T(8,128)S(1)} %fusion.49), kind=kOutput, calls=%fused_computation.75 | convolution fusion | flops 509607936 | bytes 2654208 | tf_op jit(solution)/shard_map/...ij,...jk->...ik/dot_general | solution.py:16
  49.1 1.4 %fusion.17 = f32[2,3,192,192]{3,2,1,0:T(8,128)S(1)} fusion(f32[2,3,192,192]{3,2,1,0:T(8,128)S(1)} %fusion.50, f32[192,192]{1,0:T(8,128)S(1)} %fusion.36), kind=kOutput, calls=%fused_computation.34 | convolution fusion | flops 510492672 | bytes 1916928 | tf_op jit(solution)/shard_map/...ij,...jk->...ik/dot_general | solution.py:16
  50.5 1.3 %fusion.53 = f32[2,3,192,192]{3,2,1,0:T(8,128)S(1)} fusion(f32[2,3,192,192]{3,2,1,0:T(8,128)S(1)} %fusion.17, f32[2,3,192,192]{3,2,1,0:T(8,128)S(1)} %fusion.18), kind=kOutput, calls=%fused_computation.78 | convolution fusion | flops 509607936 | bytes 2654208 | tf_op jit(solution)/shard_map/...ij,...jk->...ik/dot_general | solution.py:16
  51.8 1.3 %fusion.51 = f32[2,3,192,192]{3,2,1,0:T(8,128)S(1)} fusion(f32[2,3,192,192]{3,2,1,0:T(8,128)S(1)} %fusion.17, f32[2,3,192,192]{3,2,1,0:T(8,128)S(1)} %fusion.50), kind=kOutput, calls=%fused_computation.76 | convolution fusion | flops 509607936 | bytes 2654208 | tf_op jit(solution)/shard_map/...ij,...jk->...ik/dot_general | solution.py:16
  53.1 1.3 %fusion.52 = f32[2,3,192,192]{3,2,1,0:T(8,128)S(1)} fusion(f32[2,3,192,192]{3,2,1,0:T(8,128)S(1)} %fusion.17, f32[2,3,192,192]{3,2,1,0:T(8,128)S(1)} %fusion.51), kind=kOutput, calls=%fused_computation.77 | convolution fusion | flops 509607936 | bytes 2654208 | tf_op jit(solution)/shard_map/...ij,...jk->...ik/dot_general | solution.py:16
  54.4 1.7 %fusion.16 = f32[2,3,192,192]{3,2,1,0:T(8,128)S(1)} fusion(f32[2,3,192,192]{3,2,1,0:T(8,128)S(1)} %fusion.52, f32[192,192]{1,0:T(8,128)S(1)} %fusion.36), kind=kOutput, calls=%fused_computation.32 | convolution fusion | flops 510492672 | bytes 1916928 | tf_op jit(solution)/shard_map/...ij,...jk->...ik/dot_general | solution.py:16
  56.0 0.0 copy-start
  56.0 1.3 %fusion.19 = bf16[2,3,192,192]{3,2,1,0:T(8,128)(2,1)S(1)} fusion(f32[2,3,192,192]{3,2,1,0:T(8,128)S(1)} %fusion.16, f32[2,3,192,192]{3,2,1,0:T(8,128)S(1)} %fusion.53, f32[2,3]{1,0:T(2,128)S(1)} %get-tuple-element.9), kind=kOutput, calls=%fused_computation.37 | convolution fusion | flops 510050304 | bytes 2211864 | tf_op jit(solution)/shard_map/...ij,...jk->...ik/dot_general | solution.py:16
  57.3 16.1 %fusion.44 = (bf16[2,3,640,1280]{3,2,1,0:T(8,128)(2,1)}, f32[2,3,640,1280]{3,2,1,0:T(8,128)}) fusion(f32[2,3,640,1280]{3,2,1,0:T(8,128)} %param.9, bf16[2,3,192,192]{3,2,1,0:T(8,128)(2,1)S(1)} %fusion.19, bf16[2,1,192,640]{3,2,0,1:T(8,128)(2,1)S(1)} %copy-done, bf16[2,1,192,640]{3,2,0,1:T(8,128)(2,1)S(1)} %get-tuple-element.7, ...), kind=kOutput, calls=%fused_computation.73 | convolution fusion | flops 2474311680 | bytes 53526528 | tf_op jit(solution)/shard_map/lktd,lkth->lkdh/dot_general | solution.py:76
  73.4 2.9 %fusion.2 = f32[2,192,1280]{2,1,0:T(8,128)S(1)} fusion(bf16[2,3,640,1280]{3,2,1,0:T(8,128)(2,1)} %get-tuple-element.13, bf16[2,3,192,640]{3,2,0,1:T(8,128)(2,1)S(1)} %bitcast.104), kind=kOutput, calls=%fused_computation.8 | convolution fusion | flops 629145600 | bytes 5734400 | tf_op jit(solution)/shard_map/ltd,ldh->lth/dot_general | solution.py:58
  76.3 5.7 %fusion.20 = bf16[2,192,640]{2,1,0:T(8,128)(2,1)} fusion(bf16[2,3,640,1280]{3,2,1,0:T(8,128)(2,1)} %get-tuple-element.13, f32[2,192,1280]{2,1,0:T(8,128)S(1)} %fusion.2, bf16[2,3,192,640]{3,2,0,1:T(8,128)(2,1)S(1)} %bitcast.105), kind=kOutput, calls=%fused_computation.38 | convolution fusion | flops 1261486080 | bytes 9502720 | tf_op jit(solution)/shard_map/lth,ldh->ltd/dot_general | solution.py:84
  82.0 1.1 %copy.22 = bf16[4,2,48,640]{3,2,1,0:T(8,128)(2,1)S(1)} copy(bf16[4,2,48,640]{3,2,0,1:T(8,128)(2,1)} %bitcast.108) | data formatting | bytes 983040 | tf_op jit(solution)/shard_map/transpose | solution.py:87
  83.1 10.1 %all_to_all.10 = bf16[8,48,640]{2,1,0:T(8,128)(2,1)S(1)} all-to-all(bf16[8,48,640]{2,1,0:T(8,128)(2,1)S(1)} %bitcast.106), channel_id=1, replica_groups=mesh['dp'=8,'ctx'=4] {'ctx'}, dimensions={0} | all-to-all | bytes 983040 | tf_op jit(solution)/shard_map/all_to_all | solution.py:89
  93.2 0.9 copy.23
  (8 shorter events, 0.0 us)
Async XLA Ops:
  5.1 23.4 %all-to-all-start = ((bf16[8,3,48,640]{3,2,1,0:T(8,128)(2,1)}), bf16[8,3,48,640]{3,2,1,0:T(8,128)(2,1)S(1)}, u32[]{:S(2)}, u32[]{:S(2)}) async-start(bf16[8,3,48,640]{3,2,1,0:T(8,128)(2,1)} %maximum_bitcast_fusion), calls=%async_computation | async-start | bytes 2949120 | tf_op jit(solution)/shard_map/all_to_all | solution.py:52
  42.2 1.5 %copy-start.1 = (bf16[2,1,192,1280]{3,2,0,1:T(8,128)(2,1)}, bf16[2,1,192,1280]{3,2,0,1:T(8,128)(2,1)S(1)}, u32[]{:S(2)}) copy-start(bf16[2,1,192,1280]{3,2,0,1:T(8,128)(2,1)S(1)} %get-tuple-element.4) | copy-start | bytes 2949124
  42.2 1.5 %copy-start.2 = (bf16[2,1,192,1280]{3,2,0,1:T(8,128)(2,1)}, bf16[2,1,192,1280]{3,2,0,1:T(8,128)(2,1)S(1)}, u32[]{:S(2)}) copy-start(bf16[2,1,192,1280]{3,2,0,1:T(8,128)(2,1)S(1)} %get-tuple-element.5) | copy-start | bytes 2949124
  42.2 1.6 %copy-start.3 = (bf16[2,1,192,1280]{3,2,0,1:T(8,128)(2,1)}, bf16[2,1,192,1280]{3,2,0,1:T(8,128)(2,1)S(1)}, u32[]{:S(2)}) copy-start(bf16[2,1,192,1280]{3,2,0,1:T(8,128)(2,1)S(1)} %get-tuple-element.6) | copy-start | bytes 2949124
  56.0 1.3 %copy-start = (bf16[2,1,192,640]{3,2,0,1:T(8,128)(2,1)S(1)}, bf16[2,1,192,640]{3,2,0,1:T(8,128)(2,1)}, u32[]{:S(2)}) copy-start(bf16[2,1,192,640]{3,2,0,1:T(8,128)(2,1)} %get-tuple-element.8) | copy-start | bytes 1474564

commit v2 on v1

v2 whole, which is shorter than its diff:
```python
import functools
import math

import jax
import jax.numpy as jnp
from jax import lax
from jax.experimental import pallas as pl
from jax.experimental.pallas import tpu as pltpu
from jax.sharding import PartitionSpec as P

NS_ITERS = 3
TILE = 256
MESH = pl.DeviceIdType.MESH

linear_term = 3.4445
cubic_term = -4.775
quintic_term = 2.0315


def dot(left, right):
    return jnp.dot(left, right, preferred_element_type=jnp.float32)


def dot_rows(left, right):
    return lax.dot_general(
        left, right, (((1,), (1,)), ((), ())), preferred_element_type=jnp.float32
    )


def split(values):
    high = values.astype(jnp.bfloat16)
    return high, (values - high.astype(jnp.float32)).astype(jnp.bfloat16)


def mm(left, right):
    return dot(left[0], right[0]) + (dot(left[0], right[1]) + dot(left[1], right[0]))


def factor_chain(squares, key_grams, scales):
    size = squares[0].shape[0]
    row = lax.broadcasted_iota(jnp.int32, (size, size), 0)
    col = lax.broadcasted_iota(jnp.int32, (size, size), 1)
    eye = jnp.where(row == col, jnp.float32(linear_term), jnp.float32(0.0))
    inverses, powers = [], []
    for square, key_gram in zip(squares, key_grams):
        norm = jnp.maximum(jnp.sum(square * key_gram, keepdims=True), 0.0)
        inverses.append(lax.rsqrt(norm + 1e-06))
    key_splits = {id(g): split(g) for g in key_grams}
    for square, key_gram, inverse in zip(squares, key_grams, inverses):
        powers.append(mm(split(square * (inverse * inverse)), key_splits[id(key_gram)]))
    totals = None
    for step in range(NS_ITERS):
        parts = [split(p) for p in powers]
        squared = [mm(p, p) for p in parts]
        polys = [
            split(eye + cubic_term * p + quintic_term * s) for p, s in zip(powers, squared)
        ]
        if step < NS_ITERS - 1:
            once = [split(mm(q, p)) for q, p in zip(polys, parts)]
            powers = [mm(q, o) for q, o in zip(polys, once)]
        if totals is None:
            totals = polys
        elif step < NS_ITERS - 1:
            totals = [split(mm(q, t)) for q, t in zip(polys, totals)]
        else:
            totals = [mm(q, t) for q, t in zip(polys, totals)]
    return [t * (i * s) for t, i, s in zip(totals, inverses, scales)]


def owner_kernel(
    n, packed, weights, mixed, lefts, result,
    moved, held, rights, chain, total, send_sem, recv_sem, own_sem, weight_sem,
):
    local, width, hid = held.shape[0], held.shape[2], held.shape[3]
    tokens = n * moved.shape[3]
    me = lax.axis_index("ctx")

    loads = {}
    for l in range(local):
        for k in range(3):
            loads[l, k] = pltpu.make_async_copy(
                weights.at[l, k], held.at[l, k], weight_sem.at[l, k]
            )

    barrier = pltpu.get_barrier_semaphore()
    for j in range(1, n):
        pl.semaphore_signal(
            barrier, inc=1, device_id={"ctx": lax.rem(me + j, n)}, device_id_type=MESH
        )
    pl.semaphore_wait(barrier, n - 1)

    groups = (pl.ds(0, 2), pl.ds(2, 1))
    sends, owns = {}, {}
    for g in range(2):
        for l in range(local):
            owns[l, g] = pltpu.make_async_copy(
                packed.at[me, l, groups[g]], moved.at[me, l, groups[g]], own_sem.at[l, g]
            )
            owns[l, g].start()
            for j in range(1, n):
                target = lax.rem(me + j, n)
                sends[j, l, g] = pltpu.make_async_remote_copy(
                    src_ref=packed.at[target, l, groups[g]],
                    dst_ref=moved.at[me, l, groups[g]],
                    send_sem=send_sem.at[j - 1, l, g],
                    recv_sem=recv_sem.at[j - 1, l, g],
                    device_id={"ctx": target},
                    device_id_type=MESH,
                )
                sends[j, l, g].start()
    for l in range(local):
        for k in range(3):
            loads[l, k].start()

    def arrived(l, g):
        owns[l, g].wait()
        for j in range(1, n):
            sends[j, l, g].wait_recv()

    def rows(l, k):
        return moved[:, l, k].reshape(tokens, width)

    def columns(j):
        return pl.ds(pl.multiple_of(j * TILE, TILE), TILE)

    for l in range(local):
        arrived(l, 0)
        for k in range(3):
            loads[l, k].wait()

        @pl.loop(0, hid // TILE)
        def _(j):
            cols = columns(j)
            keys, scaled = rows(l, 0), rows(l, 1)
            gate_pre = dot(keys, held[l, 0, :, cols].astype(jnp.bfloat16))
            up_proj = dot(keys, held[l, 1, :, cols].astype(jnp.bfloat16))
            back_grad = -dot(scaled, held[l, 2, :, cols].astype(jnp.bfloat16))
            sigmoid_gate = jax.nn.sigmoid(gate_pre)
            silu_gate = gate_pre * sigmoid_gate
            rights[l, 0, :, cols] = (
                back_grad * up_proj * sigmoid_gate * (1.0 + gate_pre * (1.0 - sigmoid_gate))
            ).astype(jnp.bfloat16)
            rights[l, 1, :, cols] = (back_grad * silu_gate).astype(jnp.bfloat16)
            rights[l, 2, :, cols] = (silu_gate * up_proj).astype(jnp.bfloat16)

    step_scale = math.sqrt(width / hid)

    @pl.loop(0, local)
    def _(l):
        keys, scaled = rows(l, 0), rows(l, 1)
        lefts[l, 0] = keys.T
        lefts[l, 1] = scaled.T
        key_gram, scaled_gram = dot_rows(keys, keys), dot_rows(scaled, scaled)
        squares = [dot_rows(rights[l, k], rights[l, k]) for k in range(3)]
        factors = factor_chain(
            squares,
            [key_gram, key_gram, scaled_gram],
            [-step_scale, -step_scale, step_scale],
        )
        for k in range(3):
            chain[l, k] = factors[k].astype(jnp.bfloat16)

        @pl.loop(0, hid // TILE)
        def _(j):
            cols = columns(j)
            for k in range(3):
                mixed[l, k, :, cols] = dot(chain[l, k], rights[l, k, :, cols]).astype(
                    jnp.bfloat16
                )

    for l in range(local):
        arrived(l, 1)
        total[...] = jnp.zeros_like(total)

        @pl.loop(0, hid // TILE)
        def _(j):
            cols = columns(j)
            queries = rows(l, 2)
            applied = [
                (held[l, k, :, cols] + dot(lefts[l, k // 2], mixed[l, k, :, cols])).astype(
                    jnp.bfloat16
                )
                for k in range(3)
            ]
            gate_pre, up_proj = dot(queries, applied[0]), dot(queries, applied[1])
            hidden = (gate_pre * jax.nn.sigmoid(gate_pre) * up_proj).astype(jnp.bfloat16)
            total[...] += dot_rows(hidden, applied[2])

        result[:, l] = total[...].astype(jnp.bfloat16).reshape(result[:, l].shape)

    for copy in sends.values():
        copy.wait_send()


def owner_step(packed, fast_weights, n):
    local, _, width, hid = fast_weights.shape
    tokens = n * packed.shape[3]
    bf16, vmem = jnp.bfloat16, pl.BlockSpec(memory_space=pltpu.VMEM)
    return pl.pallas_call(
        functools.partial(owner_kernel, n),
        out_shape=(
            jax.ShapeDtypeStruct((local, 3, tokens, hid), bf16),
            jax.ShapeDtypeStruct((local, 2, width, tokens), bf16),
            jax.ShapeDtypeStruct((n, local, packed.shape[3], width), bf16),
        ),
        in_specs=[pl.BlockSpec(memory_space=pl.ANY)] * 2,
        out_specs=(vmem, vmem, vmem),
        scratch_shapes=[
            pltpu.VMEM(packed.shape, bf16),
            pltpu.VMEM(fast_weights.shape, jnp.float32),
            pltpu.VMEM((local, 3, tokens, hid), bf16),
            pltpu.VMEM((local, 3, tokens, tokens), bf16),
            pltpu.VMEM((tokens, width), jnp.float32),
            pltpu.SemaphoreType.DMA((n - 1, local, 2)),
            pltpu.SemaphoreType.DMA((n - 1, local, 2)),
            pltpu.SemaphoreType.DMA((local, 2)),
            pltpu.SemaphoreType.DMA((local, 3)),
        ],
        compiler_params=pltpu.CompilerParams(
            collective_id=0, has_side_effects=True, vmem_limit_bytes=48 * 2**20
        ),
    )(packed, fast_weights)


def update_kernel(weights, lefts, mixed, out):
    out[0, 0] = weights[0, 0] + dot(lefts[0, 0], mixed[0, 0])


def update(fast_weights, lefts, mixed):
    local, kinds, width, hid = fast_weights.shape
    tokens, half = mixed.shape[2], hid // 2
    block = pl.BlockSpec((1, 1, width, half), lambda l, k, j: (l, k, 0, j))
    return pl.pallas_call(
        update_kernel,
        grid=(local, kinds, 2),
        out_shape=jax.ShapeDtypeStruct(fast_weights.shape, jnp.float32),
        in_specs=[
            block,
            pl.BlockSpec((1, 1, width, tokens), lambda l, k, j: (l, k // 2, 0, 0)),
            pl.BlockSpec((1, 1, tokens, half), lambda l, k, j: (l, k, 0, j)),
        ],
        out_specs=block,
        compiler_params=pltpu.CompilerParams(vmem_limit_bytes=32 * 2**20),
        cost_estimate=pl.CostEstimate(
            flops=2 * fast_weights.size * tokens,
            bytes_accessed=8 * fast_weights.size + 2 * (lefts.size + mixed.size),
            transcendentals=0,
        ),
    )(fast_weights, lefts, mixed)


def body(query_rows, key_rows, value_rows, token_rates, fast_weights):
    n = lax.axis_size("ctx")
    local = fast_weights.shape[0]
    tokens, heads, width = key_rows.shape
    scaled = (
        token_rates.astype(jnp.float32)[:, :, None] * value_rows.astype(jnp.float32)
    ).astype(jnp.bfloat16)
    packed = jnp.stack([key_rows, scaled, query_rows]).transpose(2, 0, 1, 3)
    packed = packed.reshape(n, local, 3, tokens, width)
    mixed, lefts, result = owner_step(packed, fast_weights, n)
    outputs = lax.all_to_all(
        result.reshape(heads, tokens, width), "ctx", split_axis=0, concat_axis=0, tiled=True
    )
    new_weights = update(fast_weights, lefts, mixed)
    return (outputs.transpose(1, 0, 2), new_weights)


def solution(mesh):
    placed = (
        P(("dp", "ctx"), None, None),
        P(("dp", "ctx"), None, None),
        P(("dp", "ctx"), None, None),
        P(("dp", "ctx"), None),
        P("ctx", None, None, None),
    )
    return jax.shard_map(
        body,
        mesh=mesh,
        in_specs=placed,
        out_specs=(P(("dp", "ctx"), None, None), P(("dp", "ctx"), None, None, None)),
        check_vma=False,
    )
```

time: 94.6 us -> 69 us (0.73)
  Pallas kernels: 0 us -> 57.4 us
  matrix products: 52.3 us -> 0 us
  waiting for transfers between devices: 18.2 us -> 0.01 us
  blocking collectives: 10.1 us -> 0 us
  other arithmetic: 4.03 us -> 2.55 us
  starting transfers between devices: 5.16 us -> 3.68 us
    pallas_call x0 -> x2, Pallas kernels: none -> 57.4 us  [the longest x1 38.6 us: owner_step(): pl.pallas_call(functools.partial(owner_kernel, n), out_shape=(jax.ShapeDt...]
    dot_general x19 -> x0, matrix products: 52.3 us -> none  [the longest x1 16.1 us: body(): jnp.einsum('lktd,lkth->lkdh', lefts, mixed, preferred_element_type=jnp.fl...]
    all_to_all x1, waiting for transfers between devices: 18.2 us -> 0.01 us  [body(): lax.all_to_all(result.reshape(heads, tokens, width), 'ctx', split_axis=0,...]
    all_to_all x1 -> x0, blocking collectives: 10.1 us -> none  [body(): lax.all_to_all(result, 'ctx', split_axis=0, concat_axis=0, tiled=True)]
    unnamed x9 -> x5, local copies, waits for them, and re-layouts: 0.91 us -> 3.23 us
    all_to_all x1, starting transfers between devices: 5.16 us -> 3.68 us  [body(): lax.all_to_all(result.reshape(heads, tokens, width), 'ctx', split_axis=0,...]
    another operation x1 -> x0, local copies, waits for them, and re-layouts: 1.3 us -> none  [body(): packed = jnp.stack([key_rows, scaled, query_rows]).transpose(2, 0, 1, 3)]
  transfers between devices with their start and end apart: 1 -> 1, of which waited for: 1 -> 0; matrix products, arithmetic and copies ran while one was open for 0% -> 0% of each run, Pallas kernels for 0% -> 27%
where the time goes in v2:
time: 69 us; the launch traced here: 68.5 us
  Pallas kernels  57.4 us (83%)
  local copies, waits for them, and re-layouts  4.18 us (6%)
  starting transfers between devices  3.68 us (5%)
  other arithmetic  2.55 us (4%)
    pallas_call x1, Pallas kernels, owner_step(): pl.pallas_call(functools.partial(owner_kernel, n), out_shape=(jax.ShapeDt...  38.6 us
    pallas_call x1, Pallas kernels, update(): pl.pallas_call(update_kernel, grid=(local, kinds, 2), out_shape=jax.Shape...  18.8 us
    all_to_all x1, starting transfers between devices, body(): lax.all_to_all(result.reshape(heads, tokens, width), 'ctx', split_axis=0,...  3.68 us
    unnamed x5, local copies, waits for them, and re-layouts  3.23 us
  transfers between devices with their start and end apart: 1, of which 0 were waited for; matrix products, arithmetic and copies ran while one was open for 0% of the time, Pallas kernels for 27%

profile of v2, /device:TPU:0, one launch (start us, length us, event | category | flops | bytes accessed | tf_op | source)
XLA Modules:
  0.0 68.5 jit_solution(8036486949602001816)
XLA Ops:
  0.6 0.8 %copy.10 = f32[48,8]{1,0:T(8,128)S(1)} copy(bf16[48,8]{0,1:T(8,128)(2,1)} %param.8) | data formatting | bytes 2304 | tf_op jit(solution)/shard_map/convert_element_type | solution.py:257
  1.4 1.2 %fusion = bf16[1,48,8,640]{3,2,1,0:T(8,128)(2,1)S(1)} fusion(bf16[48,8,640]{2,1,0:T(8,128)(2,1)} %param.7, f32[48,8]{1,0:T(8,128)S(1)} %copy.10), kind=kLoop, calls=%fused_computation.2 | loop fusion | flops 737280 | bytes 984576 | tf_op jit(solution)/shard_map/stack | solution.py:259
  2.6 1.4 %maximum_bitcast_fusion = bf16[8,3,48,640]{3,0,2,1:T(8,128)(2,1)S(1)} fusion(bf16[1,48,8,640]{3,2,1,0:T(8,128)(2,1)} %bitcast.11, bf16[1,48,8,640]{3,2,1,0:T(8,128)(2,1)S(1)} %fusion, bf16[1,48,8,640]{3,2,1,0:T(8,128)(2,1)} %bitcast.12), kind=kLoop, calls=%fused_computation | loop fusion | flops 1474560 | bytes 2949120 | tf_op jit(solution)/shard_map/transpose | solution.py:259
  4.0 0.2 copy.11
  4.1 38.6 %shard_map.68 = (bf16[2,3,192,1280]{3,2,1,0:T(8,128)(2,1)S(1)}, bf16[2,2,640,192]{3,2,1,0:T(8,128)(2,1)S(1)}, bf16[4,2,48,640]{3,2,1,0:T(8,128)(2,1)}) custom-call(bf16[4,2,3,48,640]{4,3,2,1,0:T(8,128)(2,1)S(1)} %bitcast.9, f32[2,3,640,1280]{3,2,1,0:T(8,128)} %weights.3), custom_call_target="tpu_custom_call" | custom-call | tf_op jit(solution)/shard_map/pallas_call | solution.py:199
  42.8 0.0 copy-start
  42.8 1.0 %copy-done = bf16[2,2,640,192]{3,2,1,0:T(8,128)(2,1)} copy-done((bf16[2,2,640,192]{3,2,1,0:T(8,128)(2,1)}, bf16[2,2,640,192]{3,2,1,0:T(8,128)(2,1)S(1)}, u32[]{:S(2)}) %copy-start) | copy-done | bytes 983064
  43.8 3.7 %all-to-all-start = ((bf16[8,48,640]{2,1,0:T(8,128)(2,1)}), bf16[8,48,640]{2,1,0:T(8,128)(2,1)S(1)}, u32[]{:S(2)}, u32[]{:S(2)}) async-start(bf16[8,48,640]{2,1,0:T(8,128)(2,1)} %bitcast.5), calls=%async_computation | async-start | bytes 983040 | tf_op jit(solution)/shard_map/all_to_all | solution.py:262
  47.5 0.0 copy-start.1
  47.5 1.3 %copy-done.1 = bf16[2,2,640,192]{3,2,1,0:T(8,128)(2,1)S(1)} copy-done((bf16[2,2,640,192]{3,2,1,0:T(8,128)(2,1)S(1)}, bf16[2,2,640,192]{3,2,1,0:T(8,128)(2,1)}, u32[]{:S(2)}) %copy-start.1) | copy-done | bytes 983064
  48.8 18.8 %shard_map.69 = f32[2,3,640,1280]{3,2,1,0:T(8,128)} custom-call(f32[2,3,640,1280]{3,2,1,0:T(8,128)} %weights.3, bf16[2,2,640,192]{3,2,1,0:T(8,128)(2,1)S(1)} %copy-done.1, bf16[2,3,192,1280]{3,2,1,0:T(8,128)(2,1)S(1)} %get-tuple-element.7.mixed), custom_call_target="tpu_custom_call" | custom-call | flops 1887436800 | bytes 43253760 | tf_op jit(solution)/shard_map/pallas_call | solution.py:233
  67.7 0.0 all-to-all-done
  67.7 0.9 %copy.12 = bf16[48,8,640]{2,1,0:T(8,128)(2,1)} copy(bf16[48,8,640]{2,0,1:T(8,128)(2,1)S(1)} %bitcast.10) | data formatting | bytes 983040
Async XLA Ops:
  42.8 1.1 %copy-start = (bf16[2,2,640,192]{3,2,1,0:T(8,128)(2,1)}, bf16[2,2,640,192]{3,2,1,0:T(8,128)(2,1)S(1)}, u32[]{:S(2)}) copy-start(bf16[2,2,640,192]{3,2,1,0:T(8,128)(2,1)S(1)} %get-tuple-element.6.lefts) | copy-start | bytes 2949124
  43.8 23.8 %all-to-all-start = ((bf16[8,48,640]{2,1,0:T(8,128)(2,1)}), bf16[8,48,640]{2,1,0:T(8,128)(2,1)S(1)}, u32[]{:S(2)}, u32[]{:S(2)}) async-start(bf16[8,48,640]{2,1,0:T(8,128)(2,1)} %bitcast.5), calls=%async_computation | async-start | bytes 983040 | tf_op jit(solution)/shard_map/all_to_all | solution.py:262
  47.5 1.3 %copy-start.1 = (bf16[2,2,640,192]{3,2,1,0:T(8,128)(2,1)S(1)}, bf16[2,2,640,192]{3,2,1,0:T(8,128)(2,1)}, u32[]{:S(2)}) copy-start(bf16[2,2,640,192]{3,2,1,0:T(8,128)(2,1)} %copy-done) | copy-start | bytes 2949124

commit v3 on v2

--- a/solution.py
+++ b/solution.py
@@ -68,8 +68,8 @@
 
 
 def owner_kernel(
-    n, packed, weights, mixed, lefts, result,
-    moved, held, rights, chain, total, send_sem, recv_sem, own_sem, weight_sem,
+    n, packed, weights, held, result,
+    moved, mixed, lefts, rights, chain, total, send_sem, recv_sem, own_sem, weight_sem,
 ):
     local, width, hid = held.shape[0], held.shape[2], held.shape[3]
     tokens = n * moved.shape[3]
@@ -123,6 +123,7 @@
     def columns(j):
         return pl.ds(pl.multiple_of(j * TILE, TILE), TILE)
 
+    step_scale = math.sqrt(width / hid)
     for l in range(local):
         arrived(l, 0)
         for k in range(3):
@@ -143,10 +144,6 @@
             rights[l, 1, :, cols] = (back_grad * silu_gate).astype(jnp.bfloat16)
             rights[l, 2, :, cols] = (silu_gate * up_proj).astype(jnp.bfloat16)
 
-    step_scale = math.sqrt(width / hid)
-
-    @pl.loop(0, local)
-    def _(l):
         keys, scaled = rows(l, 0), rows(l, 1)
         lefts[l, 0] = keys.T
         lefts[l, 1] = scaled.T
@@ -176,12 +173,11 @@
         def _(j):
             cols = columns(j)
             queries = rows(l, 2)
-            applied = [
-                (held[l, k, :, cols] + dot(lefts[l, k // 2], mixed[l, k, :, cols])).astype(
-                    jnp.bfloat16
-                )
-                for k in range(3)
-            ]
+            applied = []
+            for k in range(3):
+                updated = held[l, k, :, cols] + dot(lefts[l, k // 2], mixed[l, k, :, cols])
+                held[l, k, :, cols] = updated
+                applied.append(updated.astype(jnp.bfloat16))
             gate_pre, up_proj = dot(queries, applied[0]), dot(queries, applied[1])
             hidden = (gate_pre * jax.nn.sigmoid(gate_pre) * up_proj).astype(jnp.bfloat16)
             total[...] += dot_rows(hidden, applied[2])
@@ -199,15 +195,15 @@
     return pl.pallas_call(
         functools.partial(owner_kernel, n),
         out_shape=(
-            jax.ShapeDtypeStruct((local, 3, tokens, hid), bf16),
-            jax.ShapeDtypeStruct((local, 2, width, tokens), bf16),
+            pltpu.VMEM(fast_weights.shape, jnp.float32),
             jax.ShapeDtypeStruct((n, local, packed.shape[3], width), bf16),
         ),
         in_specs=[pl.BlockSpec(memory_space=pl.ANY)] * 2,
-        out_specs=(vmem, vmem, vmem),
+        out_specs=(vmem, vmem),
         scratch_shapes=[
             pltpu.VMEM(packed.shape, bf16),
-            pltpu.VMEM(fast_weights.shape, jnp.float32),
+            pltpu.VMEM((local, 3, tokens, hid), bf16),
+            pltpu.VMEM((local, 2, width, tokens), bf16),
             pltpu.VMEM((local, 3, tokens, hid), bf16),
             pltpu.VMEM((local, 3, tokens, tokens), bf16),
             pltpu.VMEM((tokens, width), jnp.float32),
@@ -217,36 +213,35 @@
             pltpu.SemaphoreType.DMA((local, 3)),
         ],
         compiler_params=pltpu.CompilerParams(
-            collective_id=0, has_side_effects=True, vmem_limit_bytes=48 * 2**20
+            collective_id=0, has_side_effects=True, vmem_limit_bytes=24 * 2**20
         ),
     )(packed, fast_weights)
 
 
-def update_kernel(weights, lefts, mixed, out):
-    out[0, 0] = weights[0, 0] + dot(lefts[0, 0], mixed[0, 0])
-
-
-def update(fast_weights, lefts, mixed):
-    local, kinds, width, hid = fast_weights.shape
-    tokens, half = mixed.shape[2], hid // 2
-    block = pl.BlockSpec((1, 1, width, half), lambda l, k, j: (l, k, 0, j))
+def store_kernel(held, out, sems):
+    copies = [
+        pltpu.make_async_copy(held.at[l, k], out.at[l, k], sems.at[l, k])
+        for l in range(held.shape[0])
+        for k in range(held.shape[1])
+    ]
+    for copy in copies:
+        copy.start()
+    for copy in copies:
+        copy.wait()
+
+
+def store(held):
     return pl.pallas_call(
-        update_kernel,
-        grid=(local, kinds, 2),
-        out_shape=jax.ShapeDtypeStruct(fast_weights.shape, jnp.float32),
-        in_specs=[
-            block,
-            pl.BlockSpec((1, 1, width, tokens), lambda l, k, j: (l, k // 2, 0, 0)),
-            pl.BlockSpec((1, 1, tokens, half), lambda l, k, j: (l, k, 0, j)),
-        ],
-        out_specs=block,
-        compiler_params=pltpu.CompilerParams(vmem_limit_bytes=32 * 2**20),
+        store_kernel,
+        out_shape=jax.ShapeDtypeStruct(held.shape, held.dtype),
+        in_specs=[pl.BlockSpec(memory_space=pltpu.VMEM)],
+        out_specs=pl.BlockSpec(memory_space=pl.ANY),
+        scratch_shapes=[pltpu.SemaphoreType.DMA(held.shape[:2])],
+        compiler_params=pltpu.CompilerParams(vmem_limit_bytes=8 * 2**20),
         cost_estimate=pl.CostEstimate(
-            flops=2 * fast_weights.size * tokens,
-            bytes_accessed=8 * fast_weights.size + 2 * (lefts.size + mixed.size),
-            transcendentals=0,
+            flops=0, bytes_accessed=8 * held.size, transcendentals=0
         ),
-    )(fast_weights, lefts, mixed)
+    )(held)
 
 
 def body(query_rows, key_rows, value_rows, token_rates, fast_weights):
@@ -258,11 +253,11 @@
     ).astype(jnp.bfloat16)
     packed = jnp.stack([key_rows, scaled, query_rows]).transpose(2, 0, 1, 3)
     packed = packed.reshape(n, local, 3, tokens, width)
-    mixed, lefts, result = owner_step(packed, fast_weights, n)
+    held, result = owner_step(packed, fast_weights, n)
     outputs = lax.all_to_all(
         result.reshape(heads, tokens, width), "ctx", split_axis=0, concat_axis=0, tiled=True
     )
-    new_weights = update(fast_weights, lefts, mixed)
+    new_weights = store(held)
     return (outputs.transpose(1, 0, 2), new_weights)
 
 

time: 69 us -> 65.3 us (0.946)
  Pallas kernels: 57.4 us -> 42.8 us
  local copies, waits for them, and re-layouts: 4.18 us -> 15.5 us
    pallas_call x2, Pallas kernels: 57.4 us -> 42.8 us  [the longest x1 35.9 us: owner_step(): pl.pallas_call(functools.partial(owner_kernel, n), out_shape=(pltpu.VMEM(...]
    unnamed x5, local copies, waits for them, and re-layouts: 3.23 us -> 14.6 us
  transfers between devices with their start and end apart: 1 -> 1, of which waited for: 0 -> 0; matrix products, arithmetic and copies ran while one was open for 0% -> 0% of each run, Pallas kernels for 27% -> 11%
where the time goes in v3:
time: 65.3 us; the launch traced here: 65 us
  Pallas kernels  42.8 us (66%)
  local copies, waits for them, and re-layouts  15.5 us (24%)
  starting transfers between devices  3.47 us (5%)
  other arithmetic  2.55 us (4%)
  between operations  0.7 us (1%)
    pallas_call x1, Pallas kernels, owner_step(): pl.pallas_call(functools.partial(owner_kernel, n), out_shape=(pltpu.VMEM(...  35.9 us
    unnamed x5, local copies, waits for them, and re-layouts  14.6 us
    pallas_call x1, Pallas kernels, store(): pl.pallas_call(store_kernel, out_shape=jax.ShapeDtypeStruct(held.shape, h...  6.87 us
    all_to_all x1, starting transfers between devices, body(): lax.all_to_all(result.reshape(heads, tokens, width), 'ctx', split_axis=0,...  3.47 us
    transpose x1, other arithmetic, body(): packed = jnp.stack([key_rows, scaled, query_rows]).transpose(2, 0, 1, 3)  1.37 us
  transfers between devices with their start and end apart: 1, of which 0 were waited for; matrix products, arithmetic and copies ran while one was open for 0% of the time, Pallas kernels for 11%

profile of v3, /device:TPU:0, one launch (start us, length us, event | category | flops | bytes accessed | tf_op | source)
XLA Modules:
  0.0 65.0 jit_solution(2651051867682610097)
XLA Ops:
  0.6 0.8 %copy.10 = f32[48,8]{1,0:T(8,128)S(1)} copy(bf16[48,8]{0,1:T(8,128)(2,1)} %param.8) | data formatting | bytes 2304 | tf_op jit(solution)/shard_map/convert_element_type | solution.py:252
  1.4 1.2 %fusion = bf16[1,48,8,640]{3,2,1,0:T(8,128)(2,1)S(1)} fusion(bf16[48,8,640]{2,1,0:T(8,128)(2,1)} %param.7, f32[48,8]{1,0:T(8,128)S(1)} %copy.10), kind=kLoop, calls=%fused_computation.2 | loop fusion | flops 737280 | bytes 984576 | tf_op jit(solution)/shard_map/stack | solution.py:254
  2.6 1.4 %maximum_bitcast_fusion = bf16[8,3,48,640]{3,0,2,1:T(8,128)(2,1)S(1)} fusion(bf16[1,48,8,640]{3,2,1,0:T(8,128)(2,1)} %bitcast.11, bf16[1,48,8,640]{3,2,1,0:T(8,128)(2,1)S(1)} %fusion, bf16[1,48,8,640]{3,2,1,0:T(8,128)(2,1)} %bitcast.12), kind=kLoop, calls=%fused_computation | loop fusion | flops 1474560 | bytes 2949120 | tf_op jit(solution)/shard_map/transpose | solution.py:254
  4.0 0.2 copy.11
  4.1 35.9 %shard_map.68 = (f32[2,3,640,1280]{3,2,1,0:T(8,128)S(1)}, bf16[4,2,48,640]{3,2,1,0:T(8,128)(2,1)}) custom-call(bf16[4,2,3,48,640]{4,3,2,1,0:T(8,128)(2,1)S(1)} %bitcast.9, f32[2,3,640,1280]{3,2,1,0:T(8,128)} %weights.1), custom_call_target="tpu_custom_call" | custom-call | tf_op jit(solution)/shard_map/pallas_call | solution.py:195
  40.1 0.0 copy-start
  40.1 7.1 %copy-done = f32[2,3,640,1280]{3,2,1,0:T(8,128)} copy-done((f32[2,3,640,1280]{3,2,1,0:T(8,128)}, f32[2,3,640,1280]{3,2,1,0:T(8,128)S(1)}, u32[]{:S(2)}) %copy-start) | copy-done | bytes 19660824
  47.2 3.5 %all-to-all-start = ((bf16[8,48,640]{2,1,0:T(8,128)(2,1)}), bf16[8,48,640]{2,1,0:T(8,128)(2,1)S(1)}, u32[]{:S(2)}, u32[]{:S(2)}) async-start(bf16[8,48,640]{2,1,0:T(8,128)(2,1)} %bitcast.5), calls=%async_computation | async-start | bytes 983040 | tf_op jit(solution)/shard_map/all_to_all | solution.py:257
  50.7 0.0 copy-start.1
  50.7 6.6 %copy-done.1 = f32[2,3,640,1280]{3,2,1,0:T(8,128)S(1)} copy-done((f32[2,3,640,1280]{3,2,1,0:T(8,128)S(1)}, f32[2,3,640,1280]{3,2,1,0:T(8,128)}, u32[]{:S(2)}) %copy-start.1) | copy-done | bytes 19660824
  57.3 6.9 %shard_map.69 = f32[2,3,640,1280]{3,2,1,0:T(8,128)} custom-call(f32[2,3,640,1280]{3,2,1,0:T(8,128)S(1)} %copy-done.1), custom_call_target="tpu_custom_call" | custom-call | bytes 39321600 | tf_op jit(solution)/shard_map/pallas_call | solution.py:234
  64.2 0.0 all-to-all-done
  64.2 0.9 %copy.12 = bf16[48,8,640]{2,1,0:T(8,128)(2,1)} copy(bf16[48,8,640]{2,0,1:T(8,128)(2,1)S(1)} %bitcast.10) | data formatting | bytes 983040
Async XLA Ops:
  40.1 7.1 %copy-start = (f32[2,3,640,1280]{3,2,1,0:T(8,128)}, f32[2,3,640,1280]{3,2,1,0:T(8,128)S(1)}, u32[]{:S(2)}) copy-start(f32[2,3,640,1280]{3,2,1,0:T(8,128)S(1)} %get-tuple-element.5.held) | copy-start | bytes 58982404
  47.2 17.0 %all-to-all-start = ((bf16[8,48,640]{2,1,0:T(8,128)(2,1)}), bf16[8,48,640]{2,1,0:T(8,128)(2,1)S(1)}, u32[]{:S(2)}, u32[]{:S(2)}) async-start(bf16[8,48,640]{2,1,0:T(8,128)(2,1)} %bitcast.5), calls=%async_computation | async-start | bytes 983040 | tf_op jit(solution)/shard_map/all_to_all | solution.py:257
  50.7 6.6 %copy-start.1 = (f32[2,3,640,1280]{3,2,1,0:T(8,128)S(1)}, f32[2,3,640,1280]{3,2,1,0:T(8,128)}, u32[]{:S(2)}) copy-start(f32[2,3,640,1280]{3,2,1,0:T(8,128)} %copy-done) | copy-start | bytes 58982404

commit v4 on v3

--- a/solution.py
+++ b/solution.py
@@ -68,8 +68,9 @@
 
 
 def owner_kernel(
-    n, packed, weights, held, result,
-    moved, mixed, lefts, rights, chain, total, send_sem, recv_sem, own_sem, weight_sem,
+    n, packed, weights, held, out,
+    moved, mixed, lefts, rights, chain, total, result, landed,
+    send_sem, recv_sem, own_sem, weight_sem, out_send_sem, out_recv_sem, out_own_sem,
 ):
     local, width, hid = held.shape[0], held.shape[2], held.shape[3]
     tokens = n * moved.shape[3]
@@ -165,6 +166,7 @@
                     jnp.bfloat16
                 )
 
+    returns = {}
     for l in range(local):
         arrived(l, 1)
         total[...] = jnp.zeros_like(total)
@@ -182,10 +184,28 @@
             hidden = (gate_pre * jax.nn.sigmoid(gate_pre) * up_proj).astype(jnp.bfloat16)
             total[...] += dot_rows(hidden, applied[2])
 
-        result[:, l] = total[...].astype(jnp.bfloat16).reshape(result[:, l].shape)
+        result[:, l] = total[...].astype(jnp.bfloat16).reshape(n, tokens // n, width)
+        returns[0, l] = pltpu.make_async_copy(
+            result.at[me, l], landed.at[me, l], out_own_sem.at[l]
+        )
+        returns[0, l].start()
+        for j in range(1, n):
+            target = lax.rem(me + j, n)
+            returns[j, l] = pltpu.make_async_remote_copy(
+                src_ref=result.at[target, l],
+                dst_ref=landed.at[me, l],
+                send_sem=out_send_sem.at[j - 1, l],
+                recv_sem=out_recv_sem.at[j - 1, l],
+                device_id={"ctx": target},
+                device_id_type=MESH,
+            )
+            returns[j, l].start()
 
     for copy in sends.values():
         copy.wait_send()
+    for copy in returns.values():
+        copy.wait()
+    out[...] = landed[...]
 
 
 def owner_step(packed, fast_weights, n):
@@ -207,10 +227,15 @@
             pltpu.VMEM((local, 3, tokens, hid), bf16),
             pltpu.VMEM((local, 3, tokens, tokens), bf16),
             pltpu.VMEM((tokens, width), jnp.float32),
+            pltpu.VMEM((n, local, packed.shape[3], width), bf16),
+            pltpu.VMEM((n, local, packed.shape[3], width), bf16),
             pltpu.SemaphoreType.DMA((n - 1, local, 2)),
             pltpu.SemaphoreType.DMA((n - 1, local, 2)),
             pltpu.SemaphoreType.DMA((local, 2)),
             pltpu.SemaphoreType.DMA((local, 3)),
+            pltpu.SemaphoreType.DMA((n - 1, local)),
+            pltpu.SemaphoreType.DMA((n - 1, local)),
+            pltpu.SemaphoreType.DMA((local,)),
         ],
         compiler_params=pltpu.CompilerParams(
             collective_id=0, has_side_effects=True, vmem_limit_bytes=24 * 2**20
@@ -253,11 +278,9 @@
     ).astype(jnp.bfloat16)
     packed = jnp.stack([key_rows, scaled, query_rows]).transpose(2, 0, 1, 3)
     packed = packed.reshape(n, local, 3, tokens, width)
-    held, result = owner_step(packed, fast_weights, n)
-    outputs = lax.all_to_all(
-        result.reshape(heads, tokens, width), "ctx", split_axis=0, concat_axis=0, tiled=True
-    )
+    held, outputs = owner_step(packed, fast_weights, n)
     new_weights = store(held)
+    outputs = outputs.reshape(heads, tokens, width)
     return (outputs.transpose(1, 0, 2), new_weights)
 
 

time: 65.3 us -> 51.9 us (0.79)
  local copies, waits for them, and re-layouts: 15.5 us -> 1.81 us
  Pallas kernels: 42.8 us -> 46.7 us
  starting transfers between devices: 3.47 us -> 0 us
    unnamed x5 -> x0, local copies, waits for them, and re-layouts: 14.6 us -> none
    pallas_call x1, Pallas kernels: 35.9 us -> 39.8 us  [owner_step(): pl.pallas_call(functools.partial(owner_kernel, n), out_shape=(pltpu.VMEM(...]
    all_to_all x1 -> x0, starting transfers between devices: 3.47 us -> none  [body(): lax.all_to_all(result.reshape(heads, tokens, width), 'ctx', split_axis=0,...]
    reshape x0 -> x1, local copies, waits for them, and re-layouts: none -> 0.87 us  [body(): outputs = outputs.reshape(heads, tokens, width)]
  transfers between devices with their start and end apart: 1 -> 0, of which waited for: 0 -> 0; matrix products, arithmetic and copies ran while one was open for 0% -> 0% of each run, Pallas kernels for 11% -> 0%
where the time goes in v4:
time: 51.9 us; the launch traced here: 51.7 us
  Pallas kernels  46.7 us (90%)
  other arithmetic  2.55 us (5%)
  local copies, waits for them, and re-layouts  1.81 us (3%)
  between operations  0.66 us (1%)
    pallas_call x1, Pallas kernels, owner_step(): pl.pallas_call(functools.partial(owner_kernel, n), out_shape=(pltpu.VMEM(...  39.8 us
    pallas_call x1, Pallas kernels, store(): pl.pallas_call(store_kernel, out_shape=jax.ShapeDtypeStruct(held.shape, h...  6.87 us
    transpose x1, other arithmetic, body(): packed = jnp.stack([key_rows, scaled, query_rows]).transpose(2, 0, 1, 3)  1.37 us
    another operation x1, other arithmetic, body(): packed = jnp.stack([key_rows, scaled, query_rows]).transpose(2, 0, 1, 3)  1.18 us

profile of v4, /device:TPU:0, one launch (start us, length us, event | category | flops | bytes accessed | tf_op | source)
XLA Modules:
  0.0 51.7 jit_solution(11265060566954569656)
XLA Ops:
  0.6 0.8 %copy.7 = f32[48,8]{1,0:T(8,128)S(1)} copy(bf16[48,8]{0,1:T(8,128)(2,1)} %param.8) | data formatting | bytes 2304 | tf_op jit(solution)/shard_map/convert_element_type | solution.py:277
  1.4 1.2 %fusion = bf16[1,48,8,640]{3,2,1,0:T(8,128)(2,1)S(1)} fusion(bf16[48,8,640]{2,1,0:T(8,128)(2,1)} %param.7, f32[48,8]{1,0:T(8,128)S(1)} %copy.7), kind=kLoop, calls=%fused_computation.2 | loop fusion | flops 737280 | bytes 984576 | tf_op jit(solution)/shard_map/stack | solution.py:279
  2.6 1.4 %maximum_bitcast_fusion = bf16[8,3,48,640]{3,0,2,1:T(8,128)(2,1)S(1)} fusion(bf16[1,48,8,640]{3,2,1,0:T(8,128)(2,1)} %bitcast.13, bf16[1,48,8,640]{3,2,1,0:T(8,128)(2,1)S(1)} %fusion, bf16[1,48,8,640]{3,2,1,0:T(8,128)(2,1)} %bitcast.14), kind=kLoop, calls=%fused_computation | loop fusion | flops 1474560 | bytes 2949120 | tf_op jit(solution)/shard_map/transpose | solution.py:279
  4.0 0.2 copy.8
  4.1 39.8 %shard_map.68 = (f32[2,3,640,1280]{3,2,1,0:T(8,128)S(1)}, bf16[4,2,48,640]{3,2,1,0:T(8,128)(2,1)S(1)}) custom-call(bf16[4,2,3,48,640]{4,3,2,1,0:T(8,128)(2,1)S(1)} %bitcast.11, f32[2,3,640,1280]{3,2,1,0:T(8,128)} %weights.1), custom_call_target="tpu_custom_call" | custom-call | tf_op jit(solution)/shard_map/pallas_call | solution.py:215
  44.0 0.9 %copy.11 = bf16[8,48,640]{2,0,1:T(8,128)(2,1)} copy(bf16[8,48,640]{2,1,0:T(8,128)(2,1)S(1)} %bitcast.12) | data formatting | bytes 983040 | tf_op jit(solution)/shard_map/reshape | solution.py:283
  44.8 6.9 %shard_map.69 = f32[2,3,640,1280]{3,2,1,0:T(8,128)} custom-call(f32[2,3,640,1280]{3,2,1,0:T(8,128)S(1)} %get-tuple-element.5.held), custom_call_target="tpu_custom_call" | custom-call | bytes 39321600 | tf_op jit(solution)/shard_map/pallas_call | solution.py:259
